TPU v7x, 128 devices: a whole 4x4x4 slice. The times are simulated.
128 devices in a mesh: ctx: 16 (over z, x_hi, core), head: 8 (over y, x_lo).
Axes of the slice: x: 4 (x_hi: 2, x_lo: 2; x = x_hi * 2 + x_lo), y: 4, z: 4, core: 2. Of those that a mesh axis runs over, the one named last changes fastest.
Arguments:
- queries: bfloat16 [2048, 8192], P('ctx', 'head'), may hold values from -17.5 to 17.5
- incoming_keys: bfloat16 [2048, 1024], P('ctx', 'head'), may hold values from -7.5 to 7.5
- incoming_values: bfloat16 [2048, 1024], P('ctx', 'head'), may hold values from -6 to 6
- paged_key_cache: bfloat16 [256, 8, 128, 128], P('ctx', 'head'), may hold values from -7.5 to 7.5
- paged_value_cache: bfloat16 [256, 8, 128, 128], P('ctx', 'head'), may hold values from -6 to 6
- block_table: int32 [4, 64], replicated, may hold values from 0 to 255, as said below
- cache_len: int32 [4], replicated, may hold values from 2048 to 8192
- new_start: int32 [5], replicated, may hold values from 0 to 2048, as said below
- out_weight: bfloat16 [8192, 8192], P('head'), may hold values from -0.09375 to 0.09375
Outputs:
- mixed: bfloat16 [2048, 8192], P('ctx', 'head')
Inputs may be any that keep to these rules, and one draw needn't show every extreme that they name: `block_table`: each page slot appears exactly once; row r lists the page slots of request r's pages in order. Rises strictly from new_start[0] = 0 to new_start[4] = 2048.
All inputs are finite; a program needn't handle non-finite values.
Results may differ from a plain program's by a relative error of at most 0.0055.
Values may be sent and summed in bfloat16 or wider, within the bound.
No kernel may reach another device: no remote copies, remote signals or barrier semaphores. Data moves between devices by JAX's collectives and lax.ppermute only.
A program may use at most 128 MiB of HBM per device.

v0:
```python
import math

import jax
import jax.numpy as jnp
from jax import lax
from jax.sharding import PartitionSpec as P

negative_fill = -1e30


def shifted_2(value, axis, by):
    count = lax.axis_size(axis)
    return lax.ppermute(value, axis, [(i, (i + by) % count) for i in range(count)])


def token_meta(positions, cache_len, new_start):
    requests = cache_len.shape[0]
    owners = jnp.sum((positions[:, None] >= new_start[None, 1:requests]).astype(jnp.int32), axis=1)
    onehot = (owners[:, None] == jnp.arange(requests, dtype=jnp.int32)[None, :]).astype(jnp.int32)
    shifted = jnp.sum(onehot * (cache_len - new_start[:requests])[None, :], axis=1)
    return (owners, shifted + positions)


def slot_meta(slot_ids, block_table, cache_len, page_size):
    requests, most = block_table.shape
    match = (block_table[:, :, None] == slot_ids[None, None, :]).astype(jnp.int32)
    owners = jnp.sum(match * jnp.arange(requests, dtype=jnp.int32)[:, None, None], axis=(0, 1))
    page_index = jnp.sum(match * jnp.arange(most, dtype=jnp.int32)[None, :, None], axis=(0, 1))
    limits = jnp.sum(match * cache_len[:, None, None], axis=(0, 1))
    places = page_index[:, None] * page_size + jnp.arange(page_size, dtype=jnp.int32)[None, :]
    key_owner = jnp.broadcast_to(owners[:, None], places.shape)
    return (key_owner, places, places < limits[:, None])


def attend(
    head_queries,
    keys,
    value_rows,
    query_owner,
    query_place,
    key_owner,
    key_place,
    key_live,
    scale_factor,
):
    scores = (
        jnp.einsum("qkgd,kbtd->kgqbt", head_queries, keys, preferred_element_type=jnp.float32)
        * scale_factor
    )
    allowed = (
        (query_owner[:, None, None] == key_owner[None])
        & (key_place[None] <= query_place[:, None, None])
        & key_live[None]
    )
    masked = jnp.where(allowed, scores, negative_fill)
    block_high = jnp.max(masked, axis=-1)
    weights = jnp.where(allowed, jnp.exp(masked - block_high[..., None]), 0.0)
    block_total = jnp.sum(weights, axis=-1)
    block_numer = jnp.einsum(
        "kgqbt,kbtd->kgqbd",
        weights.astype(jnp.bfloat16),
        value_rows,
        preferred_element_type=jnp.float32,
    )
    highest = jnp.max(block_high, axis=-1)
    scaled = jnp.exp(block_high - highest[..., None])
    return (
        highest,
        jnp.sum(scaled * block_total, axis=-1),
        jnp.sum(scaled[..., None] * block_numer, axis=-2),
    )


def merge_partials(earlier, later):
    highest = jnp.maximum(earlier[0], later[0])
    first_scale = jnp.exp(earlier[0] - highest)
    second_scale = jnp.exp(later[0] - highest)
    total = first_scale * earlier[1] + second_scale * later[1]
    numer = first_scale[..., None] * earlier[2] + second_scale[..., None] * later[2]
    return (highest, total, numer)


def on_device(
    queries,
    incoming_keys,
    incoming_values,
    paged_key_cache,
    paged_value_cache,
    block_table,
    cache_len,
    new_start,
    out_weight,
):
    devices_ctx = lax.axis_size("ctx")
    position = lax.axis_index("ctx")
    rows_here = queries.shape[0]
    local_pages, local_heads, page_size, head_width = paged_key_cache.shape
    query_group_width = queries.shape[1] // (local_heads * head_width)
    scale_factor = 1.0 / math.sqrt(head_width)
    total_new = rows_here * devices_ctx
    offsets = jnp.arange(rows_here, dtype=jnp.int32)
    my_owner, my_place = token_meta(position * rows_here + offsets, cache_len, new_start)
    my_queries = queries.reshape(rows_here, local_heads, query_group_width, head_width)
    state_shape = (local_heads, query_group_width, rows_here)
    initial = (
        jnp.full(state_shape, negative_fill, jnp.float32),
        jnp.zeros(state_shape, jnp.float32),
        jnp.zeros(state_shape + (head_width,), jnp.float32),
    )
    fresh_keys, fresh_values = (
        lax.all_gather(incoming_keys, "ctx", axis=0, tiled=True),
        lax.all_gather(incoming_values, "ctx", axis=0, tiled=True),
    )
    cache_keys = paged_key_cache.transpose(1, 0, 2, 3)
    cache_values = paged_value_cache.transpose(1, 0, 2, 3)
    slot_ids = position * local_pages + jnp.arange(local_pages, dtype=jnp.int32)
    cache_owner, cache_place, cache_live = slot_meta(slot_ids, block_table, cache_len, page_size)

    def visit(visiting, anchor):
        owners, places = token_meta(anchor * rows_here + offsets, cache_len, new_start)
        shaped = visiting.reshape(rows_here, local_heads, query_group_width, head_width)
        return attend(
            shaped,
            cache_keys,
            cache_values,
            owners,
            places,
            cache_owner,
            cache_place,
            cache_live,
            scale_factor,
        )

    last_anchor = (position + 1) % devices_ctx

    def advance(turn_index, carried):
        visiting, running = carried
        anchor = (position - turn_index) % devices_ctx
        running = merge_partials(running, visit(visiting, anchor))
        visiting = shifted_2(visiting, "ctx", 1)
        running = shifted_2((running[0], running[1], running[2]), "ctx", 1)
        return (visiting, running)

    visiting, running = lax.fori_loop(0, devices_ctx - 1, advance, (queries, initial))
    running = merge_partials(running, visit(visiting, last_anchor))
    cache_state = shifted_2((running[0], running[1], running[2]), "ctx", 1)
    fresh_token_blocks = total_new // page_size
    block_keys = fresh_keys.reshape(
        fresh_token_blocks, page_size, local_heads, head_width
    ).transpose(2, 0, 1, 3)
    block_values = fresh_values.reshape(
        fresh_token_blocks, page_size, local_heads, head_width
    ).transpose(2, 0, 1, 3)
    fresh_owner, fresh_place = token_meta(
        jnp.arange(total_new, dtype=jnp.int32), cache_len, new_start
    )
    own_partial = attend(
        my_queries,
        block_keys,
        block_values,
        my_owner,
        my_place,
        fresh_owner.reshape(fresh_token_blocks, page_size),
        fresh_place.reshape(fresh_token_blocks, page_size),
        jnp.ones((fresh_token_blocks, page_size), dtype=bool),
        scale_factor,
    )
    highest, total, numer = merge_partials(cache_state, own_partial)
    attended = (
        (numer / total[..., None])
        .transpose(2, 0, 1, 3)
        .reshape(rows_here, local_heads * query_group_width * head_width)
        .astype(jnp.bfloat16)
    )
    projected = jnp.dot(attended, out_weight, preferred_element_type=jnp.float32)
    return lax.psum_scatter(projected, "head", scatter_dimension=1, tiled=True).astype(jnp.bfloat16)


def solution(mesh):
    return jax.shard_map(
        on_device,
        mesh=mesh,
        in_specs=(
            P("ctx", "head"),
            P("ctx", "head"),
            P("ctx", "head"),
            P("ctx", "head", None, None),
            P("ctx", "head", None, None),
            P(),
            P(),
            P(),
            P("head", None),
        ),
        out_specs=P("ctx", "head"),
        check_vma=False,
    )
```

profile of v0, /device:TPU:6, one launch (start us, length us, event | category | flops | bytes accessed | tf_op | source)
XLA Modules:
  0.0 611.7 jit_solution(4578452584226998850)
XLA Ops:
  10.4 404.7 %while.23 = (s32[]{:T(128)}, bf16[128,1024]{1,0:T(8,128)(2,1)S(1)}, f32[1,8,128]{2,1,0:T(8,128)S(1)}, f32[1,8,128]{2,1,0:T(8,128)S(1)}, f32[1,8,128,128]{3,2,1,0...) while((s32[]{:T(128)}, bf16[128,1024]{1,0:T(8,128)(2,1)S(1)}, ...), condition=%wide.region_11.12_spmd.clone.clone, body=%wide.region_3.11_spmd.clone.clone.sunk | while | flops 1108636416 | bytes 36025632 | solution.py:144
  17.7 5.4 fusion.104
  28.6 7.8 %collective-permute-done.1 = f32[1,8,128]{2,1,0:T(8,128)S(1)} collective-permute-done((f32[1,8,128]{2,1,0:T(8,128)S(1)}, f32[1,8,128]{2,1,0:T(8,128)S(1)}, u32[]{:S(2)}, u32[]{:S(2)}) %collective-permute-start.1) | collective-permute-done | bytes 4128 | tf_op jit(solution)/shard_map/while/body/eval_jaxpr/ppermute | solution.py:13
  54.6 7.8 %collective-permute-done.1 = f32[1,8,128]{2,1,0:T(8,128)S(1)} collective-permute-done((f32[1,8,128]{2,1,0:T(8,128)S(1)}, f32[1,8,128]{2,1,0:T(8,128)S(1)}, u32[]{:S(2)}, u32[]{:S(2)}) %collective-permute-start.1) | collective-permute-done | bytes 4128 | tf_op jit(solution)/shard_map/while/body/eval_jaxpr/ppermute | solution.py:13
  80.6 7.8 %collective-permute-done.1 = f32[1,8,128]{2,1,0:T(8,128)S(1)} collective-permute-done((f32[1,8,128]{2,1,0:T(8,128)S(1)}, f32[1,8,128]{2,1,0:T(8,128)S(1)}, u32[]{:S(2)}, u32[]{:S(2)}) %collective-permute-start.1) | collective-permute-done | bytes 4128 | tf_op jit(solution)/shard_map/while/body/eval_jaxpr/ppermute | solution.py:13
  95.7 5.4 fusion.104
  107.2 7.2 %collective-permute-done.1 = f32[1,8,128]{2,1,0:T(8,128)S(1)} collective-permute-done((f32[1,8,128]{2,1,0:T(8,128)S(1)}, f32[1,8,128]{2,1,0:T(8,128)S(1)}, u32[]{:S(2)}, u32[]{:S(2)}) %collective-permute-start.1) | collective-permute-done | bytes 4128 | tf_op jit(solution)/shard_map/while/body/eval_jaxpr/ppermute | solution.py:13
  134.1 6.3 %collective-permute-done.1 = f32[1,8,128]{2,1,0:T(8,128)S(1)} collective-permute-done((f32[1,8,128]{2,1,0:T(8,128)S(1)}, f32[1,8,128]{2,1,0:T(8,128)S(1)}, u32[]{:S(2)}, u32[]{:S(2)}) %collective-permute-start.1) | collective-permute-done | bytes 4128 | tf_op jit(solution)/shard_map/while/body/eval_jaxpr/ppermute | solution.py:13
  147.7 5.4 fusion.104
  161.0 5.4 collective-permute-done.1
  199.7 5.4 fusion.104
  253.6 5.4 fusion.104
  268.7 5.8 collective-permute-done.1
  295.6 7.0 %collective-permute-done.1 = f32[1,8,128]{2,1,0:T(8,128)S(1)} collective-permute-done((f32[1,8,128]{2,1,0:T(8,128)S(1)}, f32[1,8,128]{2,1,0:T(8,128)S(1)}, u32[]{:S(2)}, u32[]{:S(2)}) %collective-permute-start.1) | collective-permute-done | bytes 4128 | tf_op jit(solution)/shard_map/while/body/eval_jaxpr/ppermute | solution.py:13
  322.5 8.3 %collective-permute-done.1 = f32[1,8,128]{2,1,0:T(8,128)S(1)} collective-permute-done((f32[1,8,128]{2,1,0:T(8,128)S(1)}, f32[1,8,128]{2,1,0:T(8,128)S(1)}, u32[]{:S(2)}, u32[]{:S(2)}) %collective-permute-start.1) | collective-permute-done | bytes 4128 | tf_op jit(solution)/shard_map/while/body/eval_jaxpr/ppermute | solution.py:13
  338.0 5.4 fusion.104
  349.4 9.5 %collective-permute-done.1 = f32[1,8,128]{2,1,0:T(8,128)S(1)} collective-permute-done((f32[1,8,128]{2,1,0:T(8,128)S(1)}, f32[1,8,128]{2,1,0:T(8,128)S(1)}, u32[]{:S(2)}, u32[]{:S(2)}) %collective-permute-start.1) | collective-permute-done | bytes 4128 | tf_op jit(solution)/shard_map/while/body/eval_jaxpr/ppermute | solution.py:13
  366.1 5.4 fusion.104
  376.3 10.7 %collective-permute-done.1 = f32[1,8,128]{2,1,0:T(8,128)S(1)} collective-permute-done((f32[1,8,128]{2,1,0:T(8,128)S(1)}, f32[1,8,128]{2,1,0:T(8,128)S(1)}, u32[]{:S(2)}, u32[]{:S(2)}) %collective-permute-start.1) | collective-permute-done | bytes 4128 | tf_op jit(solution)/shard_map/while/body/eval_jaxpr/ppermute | solution.py:13
  403.2 11.9 %collective-permute-done.1 = f32[1,8,128]{2,1,0:T(8,128)S(1)} collective-permute-done((f32[1,8,128]{2,1,0:T(8,128)S(1)}, f32[1,8,128]{2,1,0:T(8,128)S(1)}, u32[]{:S(2)}, u32[]{:S(2)}) %collective-permute-start.1) | collective-permute-done | bytes 4128 | tf_op jit(solution)/shard_map/while/body/eval_jaxpr/ppermute | solution.py:13
  429.0 39.4 %all_gather.6 = bf16[2048,128]{1,0:T(8,128)(2,1)S(1)} all-gather(bf16[128,128]{1,0:T(8,128)(2,1)S(1)} %copy-done.1), channel_id=1, replica_groups=mesh['ctx'=16,'head'=8] {'ctx'}, dimensions={0}, use_global_device_ids=true | all-gather | bytes 557056 | tf_op jit(solution)/shard_map/all_gather | solution.py:111
  473.5 25.1 %all_gather.7 = bf16[2048,128]{1,0:T(8,128)(2,1)S(1)} all-gather(bf16[128,128]{1,0:T(8,128)(2,1)S(1)} %copy-done.2), channel_id=1, replica_groups=mesh['ctx'=16,'head'=8] {'ctx'}, dimensions={0}, use_global_device_ids=true | all-gather | bytes 557056 | tf_op jit(solution)/shard_map/all_gather | solution.py:112
  503.1 10.2 %fusion.82 = f32[128,8192]{1,0:T(8,128)} fusion(bf16[128,1024]{0,1:T(8,128)(2,1)S(1)} %bitcast.268, bf16[1024,8192]{1,0:T(8,128)(2,1)} %param.19), kind=kOutput, calls=%fused_computation.131 | convolution fusion | flops 2147483648 | bytes 21233664 | tf_op jit(solution)/shard_map/dot_general | solution.py:175
  513.3 89.8 %reduce-scatter.2.cloned.1.call-done = f32[128,1024]{1,0:T(8,128)} async-done(((f32[128,8192]{1,0:T(8,128)}), f32[128,1024]{1,0:T(8,128)}) %reduce-scatter.2.cloned.1.call-update) | async-done | bytes 524304 | tf_op jit(solution)/shard_map/reduce_scatter | solution.py:176
  (411 shorter events, 299.1 us)
Async XLA Ops:
  6.5 596.5 %reduce-scatter.2.cloned.1.call-start = ((), (), s32[]{:S(2)}) async-start(), calls=%async_computation.1 | async-start | bytes 4718592 | tf_op jit(solution)/shard_map/reduce_scatter | solution.py:176
  23.4 13.1 %collective-permute-start.3 = (f32[1,8,128,128]{3,2,1,0:T(8,128)S(1)}, f32[1,8,128,128]{3,2,1,0:T(8,128)S(1)}, u32[]{:S(2)}, u32[]{:S(2)}) collective-permute-start(f32[1,8,128,128]{3,2,1,0:T(8,128)S(1)} %fusion.105), channel_id=1, source_target_pairs={{0,8},{8,16},{16,24},{24,32},{32,40},{40,48},{48,56},{56,64},{64,7... | collective-permute-start | bytes 1572872 | tf_op jit(solution)/shard_map/while/body/eval_jaxpr/ppermute | solution.py:13
  23.5 13.0 %collective-permute-start = (bf16[128,1024]{1,0:T(8,128)(2,1)S(1)}, bf16[128,1024]{1,0:T(8,128)(2,1)S(1)}, u32[]{:S(2)}, u32[]{:S(2)}) collective-permute-start(bf16[128,1024]{1,0:T(8,128)(2,1)S(1)} %copy.98), channel_id=1, source_target_pairs={{0,8},{8,16},{16,24},{24,32},{32,40},{40,48},{48,56},{56,64},{64,7... | collective-permute-start | bytes 786440 | tf_op jit(solution)/shard_map/while/body/eval_jaxpr/ppermute | solution.py:13
  49.4 13.1 %collective-permute-start.3 = (f32[1,8,128,128]{3,2,1,0:T(8,128)S(1)}, f32[1,8,128,128]{3,2,1,0:T(8,128)S(1)}, u32[]{:S(2)}, u32[]{:S(2)}) collective-permute-start(f32[1,8,128,128]{3,2,1,0:T(8,128)S(1)} %fusion.105), channel_id=1, source_target_pairs={{0,8},{8,16},{16,24},{24,32},{32,40},{40,48},{48,56},{56,64},{64,7... | collective-permute-start | bytes 1572872 | tf_op jit(solution)/shard_map/while/body/eval_jaxpr/ppermute | solution.py:13
  75.4 13.1 %collective-permute-start.3 = (f32[1,8,128,128]{3,2,1,0:T(8,128)S(1)}, f32[1,8,128,128]{3,2,1,0:T(8,128)S(1)}, u32[]{:S(2)}, u32[]{:S(2)}) collective-permute-start(f32[1,8,128,128]{3,2,1,0:T(8,128)S(1)} %fusion.105), channel_id=1, source_target_pairs={{0,8},{8,16},{16,24},{24,32},{32,40},{40,48},{48,56},{56,64},{64,7... | collective-permute-start | bytes 1572872 | tf_op jit(solution)/shard_map/while/body/eval_jaxpr/ppermute | solution.py:13
  101.4 13.1 %collective-permute-start.3 = (f32[1,8,128,128]{3,2,1,0:T(8,128)S(1)}, f32[1,8,128,128]{3,2,1,0:T(8,128)S(1)}, u32[]{:S(2)}, u32[]{:S(2)}) collective-permute-start(f32[1,8,128,128]{3,2,1,0:T(8,128)S(1)} %fusion.105), channel_id=1, source_target_pairs={{0,8},{8,16},{16,24},{24,32},{32,40},{40,48},{48,56},{56,64},{64,7... | collective-permute-start | bytes 1572872 | tf_op jit(solution)/shard_map/while/body/eval_jaxpr/ppermute | solution.py:13
  127.4 13.1 %collective-permute-start.3 = (f32[1,8,128,128]{3,2,1,0:T(8,128)S(1)}, f32[1,8,128,128]{3,2,1,0:T(8,128)S(1)}, u32[]{:S(2)}, u32[]{:S(2)}) collective-permute-start(f32[1,8,128,128]{3,2,1,0:T(8,128)S(1)} %fusion.105), channel_id=1, source_target_pairs={{0,8},{8,16},{16,24},{24,32},{32,40},{40,48},{48,56},{56,64},{64,7... | collective-permute-start | bytes 1572872 | tf_op jit(solution)/shard_map/while/body/eval_jaxpr/ppermute | solution.py:13
  153.4 13.1 %collective-permute-start.3 = (f32[1,8,128,128]{3,2,1,0:T(8,128)S(1)}, f32[1,8,128,128]{3,2,1,0:T(8,128)S(1)}, u32[]{:S(2)}, u32[]{:S(2)}) collective-permute-start(f32[1,8,128,128]{3,2,1,0:T(8,128)S(1)} %fusion.105), channel_id=1, source_target_pairs={{0,8},{8,16},{16,24},{24,32},{32,40},{40,48},{48,56},{56,64},{64,7... | collective-permute-start | bytes 1572872 | tf_op jit(solution)/shard_map/while/body/eval_jaxpr/ppermute | solution.py:13
  179.4 13.1 %collective-permute-start.3 = (f32[1,8,128,128]{3,2,1,0:T(8,128)S(1)}, f32[1,8,128,128]{3,2,1,0:T(8,128)S(1)}, u32[]{:S(2)}, u32[]{:S(2)}) collective-permute-start(f32[1,8,128,128]{3,2,1,0:T(8,128)S(1)} %fusion.105), channel_id=1, source_target_pairs={{0,8},{8,16},{16,24},{24,32},{32,40},{40,48},{48,56},{56,64},{64,7... | collective-permute-start | bytes 1572872 | tf_op jit(solution)/shard_map/while/body/eval_jaxpr/ppermute | solution.py:13
  205.4 13.9 %collective-permute-start.3 = (f32[1,8,128,128]{3,2,1,0:T(8,128)S(1)}, f32[1,8,128,128]{3,2,1,0:T(8,128)S(1)}, u32[]{:S(2)}, u32[]{:S(2)}) collective-permute-start(f32[1,8,128,128]{3,2,1,0:T(8,128)S(1)} %fusion.105), channel_id=1, source_target_pairs={{0,8},{8,16},{16,24},{24,32},{32,40},{40,48},{48,56},{56,64},{64,7... | collective-permute-start | bytes 1572872 | tf_op jit(solution)/shard_map/while/body/eval_jaxpr/ppermute | solution.py:13
  232.2 14.2 %collective-permute-start.3 = (f32[1,8,128,128]{3,2,1,0:T(8,128)S(1)}, f32[1,8,128,128]{3,2,1,0:T(8,128)S(1)}, u32[]{:S(2)}, u32[]{:S(2)}) collective-permute-start(f32[1,8,128,128]{3,2,1,0:T(8,128)S(1)} %fusion.105), channel_id=1, source_target_pairs={{0,8},{8,16},{16,24},{24,32},{32,40},{40,48},{48,56},{56,64},{64,7... | collective-permute-start | bytes 1572872 | tf_op jit(solution)/shard_map/while/body/eval_jaxpr/ppermute | solution.py:13
  259.3 15.2 %collective-permute-start.3 = (f32[1,8,128,128]{3,2,1,0:T(8,128)S(1)}, f32[1,8,128,128]{3,2,1,0:T(8,128)S(1)}, u32[]{:S(2)}, u32[]{:S(2)}) collective-permute-start(f32[1,8,128,128]{3,2,1,0:T(8,128)S(1)} %fusion.105), channel_id=1, source_target_pairs={{0,8},{8,16},{16,24},{24,32},{32,40},{40,48},{48,56},{56,64},{64,7... | collective-permute-start | bytes 1572872 | tf_op jit(solution)/shard_map/while/body/eval_jaxpr/ppermute | solution.py:13
  287.5 15.2 %collective-permute-start.3 = (f32[1,8,128,128]{3,2,1,0:T(8,128)S(1)}, f32[1,8,128,128]{3,2,1,0:T(8,128)S(1)}, u32[]{:S(2)}, u32[]{:S(2)}) collective-permute-start(f32[1,8,128,128]{3,2,1,0:T(8,128)S(1)} %fusion.105), channel_id=1, source_target_pairs={{0,8},{8,16},{16,24},{24,32},{32,40},{40,48},{48,56},{56,64},{64,7... | collective-permute-start | bytes 1572872 | tf_op jit(solution)/shard_map/while/body/eval_jaxpr/ppermute | solution.py:13
  315.6 15.2 %collective-permute-start.3 = (f32[1,8,128,128]{3,2,1,0:T(8,128)S(1)}, f32[1,8,128,128]{3,2,1,0:T(8,128)S(1)}, u32[]{:S(2)}, u32[]{:S(2)}) collective-permute-start(f32[1,8,128,128]{3,2,1,0:T(8,128)S(1)} %fusion.105), channel_id=1, source_target_pairs={{0,8},{8,16},{16,24},{24,32},{32,40},{40,48},{48,56},{56,64},{64,7... | collective-permute-start | bytes 1572872 | tf_op jit(solution)/shard_map/while/body/eval_jaxpr/ppermute | solution.py:13
  317.4 13.3 %collective-permute-start = (bf16[128,1024]{1,0:T(8,128)(2,1)S(1)}, bf16[128,1024]{1,0:T(8,128)(2,1)S(1)}, u32[]{:S(2)}, u32[]{:S(2)}) collective-permute-start(bf16[128,1024]{1,0:T(8,128)(2,1)S(1)} %copy.98), channel_id=1, source_target_pairs={{0,8},{8,16},{16,24},{24,32},{32,40},{40,48},{48,56},{56,64},{64,7... | collective-permute-start | bytes 786440 | tf_op jit(solution)/shard_map/while/body/eval_jaxpr/ppermute | solution.py:13
  343.7 15.2 %collective-permute-start.3 = (f32[1,8,128,128]{3,2,1,0:T(8,128)S(1)}, f32[1,8,128,128]{3,2,1,0:T(8,128)S(1)}, u32[]{:S(2)}, u32[]{:S(2)}) collective-permute-start(f32[1,8,128,128]{3,2,1,0:T(8,128)S(1)} %fusion.105), channel_id=1, source_target_pairs={{0,8},{8,16},{16,24},{24,32},{32,40},{40,48},{48,56},{56,64},{64,7... | collective-permute-start | bytes 1572872 | tf_op jit(solution)/shard_map/while/body/eval_jaxpr/ppermute | solution.py:13
  344.3 14.6 %collective-permute-start = (bf16[128,1024]{1,0:T(8,128)(2,1)S(1)}, bf16[128,1024]{1,0:T(8,128)(2,1)S(1)}, u32[]{:S(2)}, u32[]{:S(2)}) collective-permute-start(bf16[128,1024]{1,0:T(8,128)(2,1)S(1)} %copy.98), channel_id=1, source_target_pairs={{0,8},{8,16},{16,24},{24,32},{32,40},{40,48},{48,56},{56,64},{64,7... | collective-permute-start | bytes 786440 | tf_op jit(solution)/shard_map/while/body/eval_jaxpr/ppermute | solution.py:13
  371.8 15.2 %collective-permute-start.3 = (f32[1,8,128,128]{3,2,1,0:T(8,128)S(1)}, f32[1,8,128,128]{3,2,1,0:T(8,128)S(1)}, u32[]{:S(2)}, u32[]{:S(2)}) collective-permute-start(f32[1,8,128,128]{3,2,1,0:T(8,128)S(1)} %fusion.105), channel_id=1, source_target_pairs={{0,8},{8,16},{16,24},{24,32},{32,40},{40,48},{48,56},{56,64},{64,7... | collective-permute-start | bytes 1572872 | tf_op jit(solution)/shard_map/while/body/eval_jaxpr/ppermute | solution.py:13
  371.9 15.1 %collective-permute-start = (bf16[128,1024]{1,0:T(8,128)(2,1)S(1)}, bf16[128,1024]{1,0:T(8,128)(2,1)S(1)}, u32[]{:S(2)}, u32[]{:S(2)}) collective-permute-start(bf16[128,1024]{1,0:T(8,128)(2,1)S(1)} %copy.98), channel_id=1, source_target_pairs={{0,8},{8,16},{16,24},{24,32},{32,40},{40,48},{48,56},{56,64},{64,7... | collective-permute-start | bytes 786440 | tf_op jit(solution)/shard_map/while/body/eval_jaxpr/ppermute | solution.py:13
  399.9 15.2 %collective-permute-start.3 = (f32[1,8,128,128]{3,2,1,0:T(8,128)S(1)}, f32[1,8,128,128]{3,2,1,0:T(8,128)S(1)}, u32[]{:S(2)}, u32[]{:S(2)}) collective-permute-start(f32[1,8,128,128]{3,2,1,0:T(8,128)S(1)} %fusion.105), channel_id=1, source_target_pairs={{0,8},{8,16},{16,24},{24,32},{32,40},{40,48},{48,56},{56,64},{64,7... | collective-permute-start | bytes 1572872 | tf_op jit(solution)/shard_map/while/body/eval_jaxpr/ppermute | solution.py:13
  400.0 15.1 %collective-permute-start = (bf16[128,1024]{1,0:T(8,128)(2,1)S(1)}, bf16[128,1024]{1,0:T(8,128)(2,1)S(1)}, u32[]{:S(2)}, u32[]{:S(2)}) collective-permute-start(bf16[128,1024]{1,0:T(8,128)(2,1)S(1)} %copy.98), channel_id=1, source_target_pairs={{0,8},{8,16},{16,24},{24,32},{32,40},{40,48},{48,56},{56,64},{64,7... | collective-permute-start | bytes 786440 | tf_op jit(solution)/shard_map/while/body/eval_jaxpr/ppermute | solution.py:13
  426.9 75.5 %collective-permute-start.5 = (f32[1,8,128,128]{3,2,1,0:T(8,128)S(1)}, f32[1,8,128,128]{3,2,1,0:T(8,128)S(1)}, u32[]{:S(2)}, u32[]{:S(2)}) collective-permute-start(f32[1,8,128,128]{3,2,1,0:T(8,128)S(1)} %fusion.60), channel_id=1, source_target_pairs={{0,8},{8,16},{16,24},{24,32},{32,40},{40,48},{48,56},{56,64},{64,7... | collective-permute-start | bytes 1572872 | tf_op jit(solution)/shard_map/ppermute | solution.py:13
  427.0 75.4 %collective-permute-start.4 = (f32[1,8,128]{2,1,0:T(8,128)S(1)}, f32[1,8,128]{2,1,0:T(8,128)S(1)}, u32[]{:S(2)}, u32[]{:S(2)}) collective-permute-start(f32[1,8,128]{2,1,0:T(8,128)S(1)} %get-tuple-element.475), channel_id=1, source_target_pairs={{0,8},{8,16},{16,24},{24,32},{32,40},{40,48},{48,56},{56,64},{64,7... | collective-permute-start | bytes 12296 | tf_op jit(solution)/shard_map/ppermute | solution.py:13
  428.8 73.6 %collective-permute-start.6 = (f32[1,8,128]{2,1,0:T(8,128)S(1)}, f32[1,8,128]{2,1,0:T(8,128)S(1)}, u32[]{:S(2)}, u32[]{:S(2)}) collective-permute-start(f32[1,8,128]{2,1,0:T(8,128)S(1)} %get-tuple-element.474), channel_id=1, source_target_pairs={{0,8},{8,16},{16,24},{24,32},{32,40},{40,48},{48,56},{56,64},{64,7... | collective-permute-start | bytes 12296 | tf_op jit(solution)/shard_map/ppermute | solution.py:13
  (59 other events, 481.4 us)
Sparse Core Ops, SparseCore 0:
  513.4 89.6 reduce-scatter.1
where the time goes:
time: 614 us; the launch traced here: 612 us
  waiting for transfers between devices  200 us (33%)
  matrix products  140 us (23%)
  starting transfers between devices  103 us (17%)
  other arithmetic  76.5 us (12%)
  blocking collectives  64.5 us (11%)
  between operations  13.7 us (2%)
  local copies, waits for them, and re-layouts  13.4 us (2%)
    ppermute x63, waiting for transfers between devices, shifted_2(): lax.ppermute(value, axis, [(i, (i + by) % count) for i in range(count)])  110 us
    ppermute x63, starting transfers between devices, shifted_2(): lax.ppermute(value, axis, [(i, (i + by) % count) for i in range(count)])  103 us
    reduce_scatter x1, waiting for transfers between devices, on_device(): lax.psum_scatter(projected, 'head', scatter_dimension=1, tiled=True)  89.8 us
    dot_general x17, matrix products, attend(): jnp.einsum('kgqbt,kbtd->kgqbd', weights.astype(jnp.bfloat16), value_rows,...  88.1 us
    reduce_sum x17, other arithmetic, attend(): block_total = jnp.sum(weights, axis=-1)  48.5 us
    dot_general x17, matrix products, attend(): jnp.einsum('qkgd,kbtd->kgqbt', head_queries, keys, preferred_element_type...  41.5 us
    all_gather x1, blocking collectives, on_device(): lax.all_gather(incoming_keys, 'ctx', axis=0, tiled=True)  39.4 us
    all_gather x1, blocking collectives, on_device(): lax.all_gather(incoming_values, 'ctx', axis=0, tiled=True)  25.1 us
  transfers between devices with their start and end apart: 64, of which 17 were waited for; matrix products, arithmetic and copies ran while one was open for 1% of the time, Pallas kernels for 0%

commit v1 on v0

v1 whole, which is shorter than its diff:
```python
import functools
import math

import jax
import jax.numpy as jnp
from jax import lax
from jax.experimental import pallas as pl
from jax.experimental.pallas import tpu as pltpu
from jax.sharding import PartitionSpec as P

F32 = jnp.float32
BF16 = jnp.bfloat16
I32 = jnp.int32

MASKED = -1e30
LOWEST = -1e20
LIST = 64
TASKS = 128
FIELDS = 8
FAR = 1 << 20
VMEM_BYTES = 24 * 1024 * 1024
SMALL_VMEM_BYTES = 8 * 1024 * 1024


def smem():
    return pl.BlockSpec(memory_space=pltpu.SMEM)


def vmem():
    return pl.BlockSpec(memory_space=pltpu.VMEM)


def anywhere():
    return pl.BlockSpec(memory_space=pl.ANY)


def plan_kernel(requests, blocks, page_size, me_ref, table_ref, len_ref, start_ref, *refs):
    outs, slot_ref, code_ref, count_ref = refs[:2], refs[2], refs[3], refs[4]
    me = me_ref[0]
    spare = 2 * requests * LIST

    for r in range(requests):
        length = len_ref[r]

        def pages(i, counts, r=r, length=length):
            near, far = counts
            for u in range(4):
                j = 4 * i + u
                slot = table_ref[r, j]
                relative = (slot >> 4) ^ me
                live = length - j * page_size
                mine = (relative < 4) & (live > 0)
                is_far = relative >= 2
                at = jnp.where(is_far, (requests + r) * LIST + far, r * LIST + near)
                at = jnp.where(mine, at, spare)
                slot_ref[at] = (relative & 1) * (blocks + 1) + (slot & 15)
                code_ref[at] = jnp.minimum(live, page_size)
                one = jnp.where(mine, 1, 0)
                far_one = jnp.where(is_far, one, 0)
                near, far = near + one - far_one, far + far_one
            return near, far

        near, far = lax.fori_loop(
            0, (length + 4 * page_size - 1) // (4 * page_size), pages, (jnp.int32(0), jnp.int32(0))
        )
        count_ref[r] = near
        count_ref[requests + r] = far

    for phase in range(2):
        out = outs[phase]

        def step(item, first, phase=phase, out=out):
            k, r = item // requests, item % requests
            number = ((me // 4 + 4 - k) % 4) * 4 + me % 4
            low = number * 128
            begin, end = start_ref[r], start_ref[r + 1]
            which = phase * requests + r
            base = which * LIST
            total = count_ref[which]
            for side in range(2):
                other = me ^ (2 * phase + side)
                slot_ref[base + total] = side * (blocks + 1) + blocks
                code_ref[base + total] = -1 - other
                meets = (other <= number) & (begin < other * 128 + 128) & (end > other * 128)
                total = total + jnp.where(meets, 1, 0)
            slot_ref[base + total] = 0
            code_ref[base + total] = 0
            whole = (begin <= low) & (end >= low + 128)
            pairs = jnp.where((begin < low + 128) & (end > low), (total + 1) // 2, 0)

            def task(i, _):
                at = (first + i) * FIELDS
                one, two = code_ref[base + 2 * i], code_ref[base + 2 * i + 1]
                out[at] = k
                out[at + 1] = slot_ref[base + 2 * i]
                out[at + 2] = slot_ref[base + 2 * i + 1]
                out[at + 3] = one
                out[at + 4] = two
                out[at + 5] = jnp.where(whole & (one == page_size) & (two == page_size), 0, 1)
                out[at + 6] = low
                out[at + 7] = r
                return 0

            lax.fori_loop(0, pairs, task, 0)
            return first + pairs

        last = lax.fori_loop(0, 4 * requests, step, jnp.int32(0))
        out[TASKS * FIELDS] = last
        for extra in range(2):
            for field in range(FIELDS):
                out[(last + extra) * FIELDS + field] = 1 if field == 5 else 0


def make_plan(me, block_table, cache_len, new_start, blocks, page_size):
    requests = block_table.shape[0]
    return pl.pallas_call(
        functools.partial(plan_kernel, requests, blocks, page_size),
        out_shape=[jax.ShapeDtypeStruct((TASKS * FIELDS + 128,), I32)] * 2,
        in_specs=[smem()] * 4,
        out_specs=[smem()] * 2,
        scratch_shapes=[
            pltpu.SMEM((2 * requests * LIST + 8,), I32),
            pltpu.SMEM((2 * requests * LIST + 8,), I32),
            pltpu.SMEM((2 * requests,), I32),
        ],
        cost_estimate=pl.CostEstimate(flops=4_000_000_000, bytes_accessed=8_000_000, transcendentals=0),
        name="plan",
    )(me, block_table, cache_len, new_start)


def run_tasks(plan_ref, start_ref, qt_ref, keys_ref, values_ref, scores_ref, acc_ref, high_ref, sum_ref, scale, width):
    columns = qt_ref.shape[2]
    starts = list(range(0, columns, width))

    def score(task, place):
        at = task * FIELDS
        k = plan_ref[at]
        key_block = jnp.concatenate([keys_ref[plan_ref[at + 1]], keys_ref[plan_ref[at + 2]]], axis=0)
        for c in starts:
            scores_ref[place, :, c : c + width] = jnp.dot(
                key_block, qt_ref[k, :, c : c + width], preferred_element_type=F32
            )

    def absorb(task, place, masked):
        at = task * FIELDS
        k = plan_ref[at]
        value_block = jnp.concatenate(
            [values_ref[plan_ref[at + 1]].T, values_ref[plan_ref[at + 2]].T], axis=1
        )
        value_block = jnp.concatenate([value_block, jnp.ones((16, 256), BF16)], axis=0)
        if masked:
            low, r = plan_ref[at + 6], plan_ref[at + 7]
            begin, end = start_ref[r], start_ref[r + 1]
            row = lax.broadcasted_iota(I32, (128, 1), 0)
            rows = []
            for field in (3, 4):
                code = plan_ref[at + field]
                token = row - (code + 1) * 128
                rows.append(
                    jnp.where(
                        code >= 0,
                        jnp.where(row < code, -1, FAR),
                        jnp.where((token >= begin) & (token < end), token, FAR),
                    )
                )
            key_token = jnp.concatenate(rows, axis=0)
            token = low + lax.broadcasted_iota(I32, (1, width), 1) % 128
            query_token = jnp.where((token >= begin) & (token < end), token, -2)
        for c in starts:
            cols = slice(c, c + width)
            scores = scores_ref[place, :, cols]
            if masked:
                scores = jnp.where(key_token <= query_token, scores, MASKED)
            before = high_ref[k, :, cols]
            high = jnp.maximum(before, jnp.max(scores, axis=0, keepdims=True))
            weights = jnp.exp2(scores * scale - high * scale)
            shrink = jnp.exp2((before - high) * scale)
            part = jnp.dot(value_block, weights.astype(BF16), preferred_element_type=F32)
            high_ref[k, :, cols] = high
            sum_ref[k, :, cols] = sum_ref[k, :, cols] * shrink + part[128:129]
            acc_ref[k, :, cols] = acc_ref[k, :, cols] * shrink + part[:128]

    def step(task, place):
        masked = plan_ref[task * FIELDS + 5]

        @pl.when(masked == 0)
        def _():
            score(task + 1, 1 - place)
            absorb(task, place, False)

        @pl.when(masked != 0)
        def _():
            score(task + 1, 1 - place)
            absorb(task, place, True)

    def two(i, _):
        step(2 * i, 0)
        step(2 * i + 1, 1)
        return 0

    score(0, 0)
    lax.fori_loop(0, (plan_ref[TASKS * FIELDS] + 1) // 2, two, 0)


def clear(acc_ref, high_ref, sum_ref):
    acc_ref[...] = jnp.zeros(acc_ref.shape, F32)
    high_ref[...] = jnp.full(high_ref.shape, LOWEST, F32)
    sum_ref[...] = jnp.zeros(sum_ref.shape, F32)


def near_kernel(scale, width, plan_ref, start_ref, own_ref, near_ref, q0, q1, q2, q3, *refs):
    qt_ref, acc_ref, high_ref, sum_ref, q_ref, keys_ref, values_ref, scores_ref, sems = refs
    columns = qt_ref.shape[2]
    blocks = own_ref.shape[0] // 2
    queries = [
        pltpu.make_async_copy(ref, q_ref.at[k], sems.at[k]) for k, ref in enumerate((q0, q1, q2, q3))
    ]
    copies = []
    for side, ref in enumerate((own_ref, near_ref)):
        to = pl.ds(side * blocks, blocks)
        copies.append(pltpu.make_async_copy(ref.at[pl.ds(0, blocks)], keys_ref.at[to], sems.at[4 + side]))
        copies.append(pltpu.make_async_copy(ref.at[pl.ds(blocks, blocks)], values_ref.at[to], sems.at[6 + side]))
    for copy in queries + copies:
        copy.start()
    clear(acc_ref, high_ref, sum_ref)
    for k in range(4):
        queries[k].wait()
        for c in range(0, columns, 128):
            qt_ref[k, :, c : c + 128] = q_ref[k, :, c : c + 128].T
    for copy in copies:
        copy.wait()
    run_tasks(plan_ref, start_ref, qt_ref, keys_ref, values_ref, scores_ref, acc_ref, high_ref, sum_ref, scale, width)


def far_kernel(scale, width, plan_ref, start_ref, far_ref, near_ref, qt_in, acc_in, high_in, sum_in, *refs):
    message_refs = refs[:4]
    qt_ref, acc_ref, high_ref, sum_ref, acc_a, high_a, sum_a, keys_ref, values_ref, scores_ref, sems = refs[4:]
    columns = qt_ref.shape[2]
    heads = columns // 128
    blocks = far_ref.shape[0] // 2
    copies = [pltpu.make_async_copy(qt_in, qt_ref, sems.at[0])]
    for side, ref in enumerate((far_ref, near_ref)):
        to = pl.ds(side * blocks, blocks)
        copies.append(pltpu.make_async_copy(ref.at[pl.ds(0, blocks)], keys_ref.at[to], sems.at[1 + side]))
        copies.append(pltpu.make_async_copy(ref.at[pl.ds(blocks, blocks)], values_ref.at[to], sems.at[3 + side]))
    earlier = [
        pltpu.make_async_copy(acc_in, acc_a, sems.at[5]),
        pltpu.make_async_copy(high_in, high_a, sems.at[6]),
        pltpu.make_async_copy(sum_in, sum_a, sems.at[7]),
    ]
    for copy in copies + earlier:
        copy.start()
    clear(acc_ref, high_ref, sum_ref)
    for copy in copies:
        copy.wait()
    run_tasks(plan_ref, start_ref, qt_ref, keys_ref, values_ref, scores_ref, acc_ref, high_ref, sum_ref, scale, width)
    for copy in earlier:
        copy.wait()

    for k in range(4):
        high = jnp.maximum(high_ref[k], high_a[k])
        shrink_a = jnp.exp2((high_a[k] - high) * scale)
        shrink = jnp.exp2((high_ref[k] - high) * scale)
        total = sum_a[k] * shrink_a + sum_ref[k] * shrink
        some = total > 0.0
        safe = jnp.where(some, total, 1.0)
        inverse = jnp.where(some, 1.0 / safe, 0.0)
        level = jnp.where(some, high * scale + jnp.log2(safe), MASKED)
        factor_a, factor = shrink_a * inverse, shrink * inverse
        levels = []
        for h in range(heads):
            cols = slice(h * 128, (h + 1) * 128)
            message_refs[k][cols, :] = (
                acc_a[k, :, cols] * factor_a[:, cols] + acc_ref[k, :, cols] * factor[:, cols]
            ).astype(BF16)
            levels.append(level[:, cols])
        level = jnp.concatenate(levels, axis=0)
        one = level.astype(BF16)
        rest = level - one.astype(F32)
        two = rest.astype(BF16)
        three = (rest - two.astype(F32)).astype(BF16)
        tail = jnp.concatenate(
            [one.astype(F32), two.astype(F32), three.astype(F32), jnp.zeros_like(level)], axis=0
        )
        message_refs[k][heads * 128 :, :] = tail.astype(BF16)


def state_shapes(columns):
    return [(4, 128, columns), (4, 1, columns), (4, 1, columns)]


def key_scratch(blocks, columns):
    return [
        pltpu.VMEM((2 * blocks, 128, 128), BF16),
        pltpu.VMEM((2 * blocks, 128, 128), BF16),
        pltpu.VMEM((2, 256, columns), F32),
        pltpu.SemaphoreType.DMA((8,)),
    ]


def attend_near(plan, new_start, own, near, queries, scale):
    rows, columns = queries[0].shape
    return pl.pallas_call(
        functools.partial(near_kernel, scale, 256),
        out_shape=[jax.ShapeDtypeStruct((4, 128, columns), BF16)]
        + [jax.ShapeDtypeStruct(s, F32) for s in state_shapes(columns)],
        in_specs=[smem()] * 2 + [anywhere()] * 6,
        out_specs=[vmem()] * 4,
        scratch_shapes=[pltpu.VMEM((4, rows, columns), BF16)] + key_scratch(own.shape[0] // 2, columns),
        compiler_params=pltpu.CompilerParams(vmem_limit_bytes=VMEM_BYTES),
        cost_estimate=pl.CostEstimate(flops=8_000_000_000, bytes_accessed=8_000_000, transcendentals=4_000_000),
        name="attend_near",
    )(plan, new_start, own, near, *queries)


def attend_far(plan, new_start, far, far_near, state, scale):
    columns = state[0].shape[2]
    rows = columns + 4 * (columns // 128)
    states = [pltpu.VMEM(s, F32) for s in state_shapes(columns)]
    return pl.pallas_call(
        functools.partial(far_kernel, scale, 256),
        out_shape=[jax.ShapeDtypeStruct((rows, 128), BF16)] * 4,
        in_specs=[smem()] * 2 + [anywhere()] * 6,
        out_specs=[vmem()] * 4,
        scratch_shapes=[pltpu.VMEM((4, 128, columns), BF16)]
        + states
        + states
        + key_scratch(far.shape[0] // 2, columns),
        compiler_params=pltpu.CompilerParams(vmem_limit_bytes=VMEM_BYTES),
        cost_estimate=pl.CostEstimate(flops=8_000_000_000, bytes_accessed=8_000_000, transcendentals=4_000_000),
        name="attend_far",
    )(plan, new_start, far, far_near, *state)


def merged(messages, heads, out_ref):
    tails = [m[heads * 128 :, :].astype(F32) for m in messages]
    levels = [t[:heads] + t[heads : 2 * heads] + t[2 * heads : 3 * heads] for t in tails]
    top = functools.reduce(jnp.maximum, levels)
    weights = [jnp.exp2(level - top) for level in levels]
    total = functools.reduce(jnp.add, weights)
    weights = [w / total for w in weights]
    for h in range(heads):
        rows = slice(h * 128, (h + 1) * 128)
        value = sum(m[rows, :].astype(F32) * w[h : h + 1, :] for m, w in zip(messages, weights))
        out_ref[:, rows] = value.T.astype(BF16)


def merge_kernel(heads, *refs):
    merged(refs[:4], heads, refs[4])


def merge(messages, heads):
    return pl.pallas_call(
        functools.partial(merge_kernel, heads),
        out_shape=jax.ShapeDtypeStruct((128, heads * 128), BF16),
        in_specs=[vmem()] * 4,
        out_specs=vmem(),
        compiler_params=pltpu.CompilerParams(vmem_limit_bytes=SMALL_VMEM_BYTES),
        cost_estimate=pl.CostEstimate(flops=2_000_000, bytes_accessed=1_300_000, transcendentals=4096),
        name="merge",
    )(*messages)


def bring_kernel(wide, targets_ref, source_ref, *refs):
    outs, sems = refs[:-1], refs[-1]
    pieces = 2
    step = source_ref.shape[0] // pieces
    copies = []
    for n, out in enumerate(outs):
        at = pl.multiple_of(targets_ref[n] * wide, wide)
        for p in range(pieces):
            rows = pl.ds(p * step, step)
            copies.append(
                pltpu.make_async_copy(
                    source_ref.at[rows, pl.ds(at, wide)], out.at[rows], sems.at[n * pieces + p]
                )
            )
            copies[-1].start()
    for copy in copies:
        copy.wait()


def bring(targets, value, wide):
    count = targets.shape[0]
    depth = value.shape[0]
    return pl.pallas_call(
        functools.partial(bring_kernel, wide),
        out_shape=[jax.ShapeDtypeStruct((depth, wide), value.dtype)] * count,
        in_specs=[smem(), anywhere()],
        out_specs=[vmem()] * count,
        scratch_shapes=[pltpu.SemaphoreType.DMA((2 * count,))],
        compiler_params=pltpu.CompilerParams(vmem_limit_bytes=VMEM_BYTES),
        cost_estimate=pl.CostEstimate(flops=0, bytes_accessed=2 * value.size * 2, transcendentals=0),
        name="bring",
    )(targets, value)


def project_kernel(x_ref, w_ref, out_ref):
    out_ref[...] = jnp.dot(x_ref[...], w_ref[...], preferred_element_type=F32).astype(out_ref.dtype)


def project(attended, weight, dtype):
    rows, depth = attended.shape
    wide = weight.shape[1]
    return pl.pallas_call(
        project_kernel,
        out_shape=jax.ShapeDtypeStruct((rows, wide), dtype),
        in_specs=[vmem()] * 2,
        out_specs=vmem(),
        compiler_params=pltpu.CompilerParams(vmem_limit_bytes=SMALL_VMEM_BYTES),
        cost_estimate=pl.CostEstimate(
            flops=2 * rows * depth * wide, bytes_accessed=2 * depth * wide, transcendentals=0
        ),
        name="project",
    )(attended, weight)


def swap(value, axis, mask):
    return lax.ppermute(value, axis, [(i, i ^ mask) for i in range(lax.axis_size(axis))])


def forward(value, axis, by):
    count = lax.axis_size(axis)
    return lax.ppermute(value, axis, [(i, (i + by) % count) for i in range(count)])


def on_device(
    queries,
    incoming_keys,
    incoming_values,
    paged_key_cache,
    paged_value_cache,
    block_table,
    cache_len,
    new_start,
    out_weight,
):
    position = lax.axis_index("ctx")
    column = lax.axis_index("head")
    head_count = lax.axis_size("head")
    blocks = paged_key_cache.shape[0]
    page_size, head_width = paged_key_cache.shape[2:]
    scale = math.log2(math.e) / math.sqrt(head_width)
    wide = out_weight.shape[1] // head_count
    masks = (5, 4, 3, 7, 2, 6, 1)
    me = position.astype(I32).reshape(1)

    def as_blocks(value):
        return value.reshape(-1, page_size, head_width)

    own = jnp.concatenate(
        [as_blocks(v) for v in (paged_key_cache, incoming_keys, paged_value_cache, incoming_values)], axis=0
    )
    far = swap(own, "ctx", 2)
    near = swap(own, "ctx", 1)
    query_one = forward(queries, "ctx", 4)
    query_three = forward(queries, "ctx", 12)
    plan = make_plan(me, block_table, cache_len, new_start, blocks, page_size)
    query_two = forward(queries, "ctx", 8)
    state = attend_near(
        plan[0], new_start, own, near, [queries, query_one, query_two, query_three], scale
    )
    far, state = lax.optimization_barrier((far, state))
    far_near = swap(far, "ctx", 1)
    messages = attend_far(plan[1], new_start, far, far_near, state, scale)
    out_weight, *messages = lax.optimization_barrier([out_weight, *messages])
    weights = bring(column ^ jnp.array(masks + (0,), I32), out_weight, wide)
    received = [messages[0]] + [forward(messages[k], "ctx", -4 * k) for k in range(1, 4)]

    attended = merge(received, queries.shape[1] // head_width)
    shares = [
        swap(project(attended, weight, BF16), "head", mask) for mask, weight in zip(masks, weights)
    ]
    total = project(attended, weights[-1], F32)
    for share in shares:
        total = total + share.astype(F32)
    return total.astype(BF16)


def solution(mesh):
    return jax.shard_map(
        on_device,
        mesh=mesh,
        in_specs=(
            P("ctx", "head"),
            P("ctx", "head"),
            P("ctx", "head"),
            P("ctx", "head", None, None),
            P("ctx", "head", None, None),
            P(),
            P(),
            P(),
            P("head", None),
        ),
        out_specs=P("ctx", "head"),
        check_vma=False,
    )
```

time: 614 us -> 100 us (0.16)
  waiting for transfers between devices: 200 us -> 30 us
  matrix products: 140 us -> 0 us
  starting transfers between devices: 103 us -> 22.6 us
  other arithmetic: 76.5 us -> 2.43 us
  blocking collectives: 64.5 us -> 0 us
  Pallas kernels: 0 us -> 43.5 us
  between operations: 13.7 us -> 0.21 us
  local copies, waits for them, and re-layouts: 13.4 us -> 0.7 us
    dot_general x35 -> x0, matrix products: 140 us -> none  [the longest x17 88.1 us: attend(): jnp.einsum('kgqbt,kbtd->kgqbd', weights.astype(jnp.bfloat16), value_rows,...]
    reduce_scatter x1 -> x0, waiting for transfers between devices: 89.8 us -> none  [on_device(): lax.psum_scatter(projected, 'head', scatter_dimension=1, tiled=True)]
    ppermute x63 -> x16, starting transfers between devices: 103 us -> 22.6 us  [the longest x10 14 us: swap(): lax.ppermute(value, axis, [(i, i ^ mask) for i in range(lax.axis_size(axi...]
    ppermute x63 -> x16, waiting for transfers between devices: 110 us -> 30 us  [the longest x10 18.1 us: swap(): lax.ppermute(value, axis, [(i, i ^ mask) for i in range(lax.axis_size(axi...]
    all_gather x2 -> x0, blocking collectives: 64.5 us -> none  [the longest x1 39.4 us: on_device(): lax.all_gather(incoming_keys, 'ctx', axis=0, tiled=True)]
    reduce_sum x69 -> x0, other arithmetic: 52.9 us -> none  [the longest x17 48.5 us: attend(): block_total = jnp.sum(weights, axis=-1)]
    pallas_call x0 -> x13, Pallas kernels: none -> 43.5 us  [the longest x1 14.1 us: attend_far(): pl.pallas_call(functools.partial(far_kernel, scale, 256), out_shape=[jax....]
    and x16 -> x0, other arithmetic: 12.5 us -> none  [attend(): (query_owner[:, None, None] == key_owner[None]) & (key_place[None] <= que...]
  transfers between devices with their start and end apart: 64 -> 16, of which waited for: 17 -> 7; matrix products, arithmetic and copies ran while one was open for 1% -> 0% of each run, Pallas kernels for 0% -> 29%
where the time goes in v1:
time: 100 us; the launch traced here: 99.5 us
  Pallas kernels  43.5 us (44%)
  waiting for transfers between devices  30 us (30%)
  starting transfers between devices  22.6 us (23%)
  other arithmetic  2.43 us (2%)
    ppermute x10, waiting for transfers between devices, swap(): lax.ppermute(value, axis, [(i, i ^ mask) for i in range(lax.axis_size(axi...  18.1 us
    pallas_call x1, Pallas kernels, attend_far(): pl.pallas_call(functools.partial(far_kernel, scale, 256), out_shape=[jax....  14.1 us
    ppermute x10, starting transfers between devices, swap(): lax.ppermute(value, axis, [(i, i ^ mask) for i in range(lax.axis_size(axi...  14 us
    pallas_call x1, Pallas kernels, attend_near(): pl.pallas_call(functools.partial(near_kernel, scale, 256), out_shape=[jax...  13.3 us
    ppermute x6, waiting for transfers between devices, forward(): lax.ppermute(value, axis, [(i, (i + by) % count) for i in range(count)])  11.9 us
    ppermute x6, starting transfers between devices, forward(): lax.ppermute(value, axis, [(i, (i + by) % count) for i in range(count)])  8.6 us
    pallas_call x1, Pallas kernels, bring(): pl.pallas_call(functools.partial(bring_kernel, wide), out_shape=[jax.Shap...  6.54 us
    pallas_call x1, Pallas kernels, make_plan(): pl.pallas_call(functools.partial(plan_kernel, requests, blocks, page_size...  5.45 us
  transfers between devices with their start and end apart: 16, of which 7 were waited for; matrix products, arithmetic and copies ran while one was open for 0% of the time, Pallas kernels for 29%

profile of v1, /device:TPU:6, one launch (start us, length us, event | category | flops | bytes accessed | tf_op | source)
XLA Modules:
  0.0 99.5 jit_solution(10527692856217952271)
XLA Ops:
  0.0 1.4 %pad_maximum_fusion.own_ref = bf16[34,128,128]{2,1,0:T(8,128)(2,1)S(1)} fusion(bf16[1,128,128]{2,1,0:T(8,128)(2,1)} %bitcast.7, bf16[16,128,128]{2,1,0:T(8,128)(2,1)} %bitcast.5, bf16[1,128,128]{2,1,0:T(8,128)(2,1)} %bitcast.8, bf16[16,128,128]{2,1,0:T(8,128)(2,1)} %bitcast.6), kind=kLoop, calls=%fused_computation | loop fusion | flops 1671168 | bytes 2228224 | tf_op jit(solution)/shard_map/concatenate | solution.py:451
  1.5 1.5 %collective-permute-start = (bf16[34,128,128]{2,1,0:T(8,128)(2,1)S(1)}, bf16[34,128,128]{2,1,0:T(8,128)(2,1)S(1)}, u32[]{:S(2)}, u32[]{:S(2)}) collective-permute-start(bf16[34,128,128]{2,1,0:T(8,128)(2,1)S(1)} %pad_maximum_fusion.own_ref), channel_id=1, source_target_pairs={{0,16},{8,24},{16,0},{24,8},{32,48},{40,56},{48,32},{56,40},{64,80... | collective-permute-start | bytes 3342344 | tf_op jit(solution)/shard_map/ppermute | solution.py:419
  3.0 1.9 %collective-permute-start.2 = (bf16[128,1024]{1,0:T(8,128)(2,1)}, bf16[128,1024]{1,0:T(8,128)(2,1)}, u32[]{:S(2)}, u32[]{:S(2)}) collective-permute-start(bf16[128,1024]{1,0:T(8,128)(2,1)} %q0.1), channel_id=1, source_target_pairs={{0,32},{8,40},{16,48},{24,56},{32,64},{40,72},{48,80},{56,88},{64,... | collective-permute-start | bytes 786440 | tf_op jit(solution)/shard_map/ppermute | solution.py:424
  4.9 3.6 %collective-permute-start.3 = (bf16[128,1024]{1,0:T(8,128)(2,1)}, bf16[128,1024]{1,0:T(8,128)(2,1)}, u32[]{:S(2)}, u32[]{:S(2)}) collective-permute-start(bf16[128,1024]{1,0:T(8,128)(2,1)} %q0.1), channel_id=1, source_target_pairs={{0,64},{8,72},{16,80},{24,88},{32,96},{40,104},{48,112},{56,120},{... | collective-permute-start | bytes 786440 | tf_op jit(solution)/shard_map/ppermute | solution.py:424
  8.5 1.0 %collective-permute-start.4 = (bf16[128,1024]{1,0:T(8,128)(2,1)}, bf16[128,1024]{1,0:T(8,128)(2,1)}, u32[]{:S(2)}, u32[]{:S(2)}) collective-permute-start(bf16[128,1024]{1,0:T(8,128)(2,1)} %q0.1), channel_id=1, source_target_pairs={{0,96},{8,104},{16,112},{24,120},{32,0},{40,8},{48,16},{56,24},{64... | collective-permute-start | bytes 786440 | tf_op jit(solution)/shard_map/ppermute | solution.py:424
  9.5 5.4 %plan.1 = (s32[1152]{0:T(1024)}, s32[1152]{0:T(1024)}) custom-call(s32[1]{0:T(128)} %bitcast.me_ref, s32[4,64]{1,0:T(4,128)} %table_ref.1, s32[4]{0:T(128)} %len_ref.1, s32[5]{0:T(128)} %start_ref.5), custom_call_target="tpu_custom_call" | custom-call | flops 4000000000 | bytes 8000000 | tf_op jit(solution)/shard_map/plan/pallas_call | solution.py:116
  14.9 5.8 %collective-permute-done.3.q2 = bf16[128,1024]{1,0:T(8,128)(2,1)} collective-permute-done((bf16[128,1024]{1,0:T(8,128)(2,1)}, bf16[128,1024]{1,0:T(8,128)(2,1)}, u32[]{:S(2)}, u32[]{:S(2)}) %collective-permute-start.3) | collective-permute-done | bytes 262176 | tf_op jit(solution)/shard_map/ppermute | solution.py:424
  21.4 13.3 %attend_near.1 = (bf16[4,128,1024]{2,1,0:T(8,128)(2,1)S(1)}, f32[4,128,1024]{2,1,0:T(8,128)S(1)}, f32[4,1,1024]{2,1,0:T(1,128)S(1)}, f32[4,1,1024]{2,1,0:T(1,128)S(1)}) custom-call(s32[1152]{0:T(1024)S(1)} %copy-done.2, s32[5]{0:T(128)S(1)} %copy-done, bf16[34,128,128]{2,1,0:T(8,128)(2,1)S(1)} %pad_maximum_fusion.own_ref, ...), custom_call_target="tpu_custom_call" | custom-call | flops 8000000000 | bytes 8000000 | tf_op jit(solution)/shard_map/attend_near/pallas_call | solution.py:303
  34.9 2.7 %collective-permute-done.5.near_ref = bf16[34,128,128]{2,1,0:T(8,128)(2,1)S(1)} collective-permute-done((bf16[34,128,128]{2,1,0:T(8,128)(2,1)S(1)}, bf16[34,128,128]{2,1,0:T(8,128)(2,1)S(1)}, u32[]{:S(2)}, u32[]{:S(2)}) %collective-permute-start.5) | collective-permute-done | bytes 1114144 | tf_op jit(solution)/shard_map/ppermute | solution.py:419
  37.6 14.1 %attend_far.1 = (bf16[1056,128]{1,0:T(8,128)(2,1)S(1)}, bf16[1056,128]{1,0:T(8,128)(2,1)S(1)}, bf16[1056,128]{1,0:T(8,128)(2,1)S(1)}, bf16[1056,128]{1,0:T(8,128)(2,1)S(1)}) custom-call(s32[1152]{0:T(1024)S(1)} %copy-done.1, s32[5]{0:T(128)S(1)} %copy-done, bf16[34,128,128]{2,1,0:T(8,128)(2,1)S(1)} %collective-permute-done.far_ref, ...), custom_call_target="tpu_custom_call" | custom-call | flops 8000000000 | bytes 8000000 | tf_op jit(solution)/shard_map/attend_far/pallas_call | solution.py:320
  51.8 0.8 collective-permute-start.7
  52.6 1.2 %collective-permute-start.8 = (bf16[1056,128]{1,0:T(8,128)(2,1)S(1)}, bf16[1056,128]{1,0:T(8,128)(2,1)S(1)}, u32[]{:S(2)}, u32[]{:S(2)}) collective-permute-start(bf16[1056,128]{1,0:T(8,128)(2,1)S(1)} %get-tuple-element.51), channel_id=1, source_target_pairs={{0,32},{8,40},{16,48},{24,56},{32,64},{40,72},{48,80},{56,88},{64,... | collective-permute-start | bytes 811016 | tf_op jit(solution)/shard_map/ppermute | solution.py:424
  53.8 6.5 %bring.1 = (bf16[1024,1024]{1,0:T(8,128)(2,1)S(1)}, bf16[1024,1024]{1,0:T(8,128)(2,1)S(1)}, bf16[1024,1024]{1,0:T(8,128)(2,1)S(1)}, bf16[1024,1024]{1,0:T(8,128)...) custom-call(s32[8]{0:T(128)S(1)} %broadcast_xor_fusion.targets_ref, ...), custom_call_target="tpu_custom_call" | custom-call | bytes 33554432 | tf_op jit(solution)/shard_map/bring/pallas_call | solution.py:386
  60.4 0.8 collective-permute-done.6.refs_1_
  61.2 1.6 %collective-permute-done.7.refs_2_ = bf16[1056,128]{1,0:T(8,128)(2,1)S(1)} collective-permute-done((bf16[1056,128]{1,0:T(8,128)(2,1)S(1)}, bf16[1056,128]{1,0:T(8,128)(2,1)S(1)}, u32[]{:S(2)}, u32[]{:S(2)}) %collective-permute-start.7) | collective-permute-done | bytes 270368 | tf_op jit(solution)/shard_map/ppermute | solution.py:424
  62.9 3.7 %collective-permute-done.8.refs_3_ = bf16[1056,128]{1,0:T(8,128)(2,1)S(1)} collective-permute-done((bf16[1056,128]{1,0:T(8,128)(2,1)S(1)}, bf16[1056,128]{1,0:T(8,128)(2,1)S(1)}, u32[]{:S(2)}, u32[]{:S(2)}) %collective-permute-start.8) | collective-permute-done | bytes 270368 | tf_op jit(solution)/shard_map/ppermute | solution.py:424
  67.9 3.1 %collective-permute-start.14 = (bf16[128,1024]{1,0:T(8,128)(2,1)S(1)}, bf16[128,1024]{1,0:T(8,128)(2,1)S(1)}, u32[]{:S(2)}, u32[]{:S(2)}) collective-permute-start(bf16[128,1024]{1,0:T(8,128)(2,1)S(1)} %project.14), channel_id=1, source_target_pairs={{0,6},{1,7},{2,4},{3,5},{4,2},{5,3},{6,0},{7,1},{8,14},{9,15},{10,... | collective-permute-start | bytes 786440 | tf_op jit(solution)/shard_map/ppermute | solution.py:419
  72.1 2.6 %collective-permute-start.12 = (bf16[128,1024]{1,0:T(8,128)(2,1)S(1)}, bf16[128,1024]{1,0:T(8,128)(2,1)S(1)}, u32[]{:S(2)}, u32[]{:S(2)}) collective-permute-start(bf16[128,1024]{1,0:T(8,128)(2,1)S(1)} %project.12), channel_id=1, source_target_pairs={{0,7},{1,6},{2,5},{3,4},{4,3},{5,2},{6,1},{7,0},{8,15},{9,14},{10,... | collective-permute-start | bytes 786440 | tf_op jit(solution)/shard_map/ppermute | solution.py:419
  75.2 0.9 collective-permute-start.11
  77.1 2.6 %collective-permute-start.10 = (bf16[128,1024]{1,0:T(8,128)(2,1)S(1)}, bf16[128,1024]{1,0:T(8,128)(2,1)S(1)}, u32[]{:S(2)}, u32[]{:S(2)}) collective-permute-start(bf16[128,1024]{1,0:T(8,128)(2,1)S(1)} %project.10), channel_id=1, source_target_pairs={{0,4},{1,5},{2,6},{3,7},{4,0},{5,1},{6,2},{7,3},{8,12},{9,13},{10,... | collective-permute-start | bytes 786440 | tf_op jit(solution)/shard_map/ppermute | solution.py:419
  79.7 5.0 %collective-permute-done.14 = bf16[128,1024]{1,0:T(8,128)(2,1)S(1)} collective-permute-done((bf16[128,1024]{1,0:T(8,128)(2,1)S(1)}, bf16[128,1024]{1,0:T(8,128)(2,1)S(1)}, u32[]{:S(2)}, u32[]{:S(2)}) %collective-permute-start.14) | collective-permute-done | bytes 262176 | tf_op jit(solution)/shard_map/ppermute | solution.py:419
  84.7 2.8 %collective-permute-start.9 = (bf16[128,1024]{1,0:T(8,128)(2,1)S(1)}, bf16[128,1024]{1,0:T(8,128)(2,1)S(1)}, u32[]{:S(2)}, u32[]{:S(2)}) collective-permute-start(bf16[128,1024]{1,0:T(8,128)(2,1)S(1)} %project.9), channel_id=1, source_target_pairs={{0,5},{1,4},{2,7},{3,6},{4,1},{5,0},{6,3},{7,2},{8,13},{9,12},{10,... | collective-permute-start | bytes 786440 | tf_op jit(solution)/shard_map/ppermute | solution.py:419
  88.1 10.3 %collective-permute-done.10 = bf16[128,1024]{1,0:T(8,128)(2,1)S(1)} collective-permute-done((bf16[128,1024]{1,0:T(8,128)(2,1)S(1)}, bf16[128,1024]{1,0:T(8,128)(2,1)S(1)}, u32[]{:S(2)}, u32[]{:S(2)}) %collective-permute-start.10) | collective-permute-done | bytes 262176 | tf_op jit(solution)/shard_map/ppermute | solution.py:419
  98.4 1.0 %add_convert_fusion = bf16[128,1024]{1,0:T(8,128)(2,1)} fusion(bf16[128,1024]{1,0:T(8,128)(2,1)S(1)} %collective-permute-done.15, bf16[128,1024]{1,0:T(8,128)(2,1)S(1)} %collective-permute-done.14, bf16[128,1024]{1,0:T(8,128)(2,1)S(1)} %collective-permute-done.13, bf16[128,1024]{1,0:T(8,128)(2,1)S(1)} %collective-permute-done.12, ...), kind=kLoop, calls=%fused_computation.1 | loop fusion | flops 1966080 | bytes 2621440 | tf_op jit(solution)/shard_map/convert_element_type | solution.py:477
  (32 shorter events, 5.3 us)
Async XLA Ops:
  1.4 19.4 %collective-permute-start.1 = (bf16[34,128,128]{2,1,0:T(8,128)(2,1)S(1)}, bf16[34,128,128]{2,1,0:T(8,128)(2,1)S(1)}, u32[]{:S(2)}, u32[]{:S(2)}) collective-permute-start(bf16[34,128,128]{2,1,0:T(8,128)(2,1)S(1)} %pad_maximum_fusion.own_ref), channel_id=1, source_target_pairs={{0,8},{8,0},{16,24},{24,16},{32,40},{40,32},{48,56},{56,48},{64,72... | collective-permute-start | bytes 3342344 | tf_op jit(solution)/shard_map/ppermute | solution.py:419
  1.5 33.3 %collective-permute-start = (bf16[34,128,128]{2,1,0:T(8,128)(2,1)S(1)}, bf16[34,128,128]{2,1,0:T(8,128)(2,1)S(1)}, u32[]{:S(2)}, u32[]{:S(2)}) collective-permute-start(bf16[34,128,128]{2,1,0:T(8,128)(2,1)S(1)} %pad_maximum_fusion.own_ref), channel_id=1, source_target_pairs={{0,16},{8,24},{16,0},{24,8},{32,48},{40,56},{48,32},{56,40},{64,80... | collective-permute-start | bytes 3342344 | tf_op jit(solution)/shard_map/ppermute | solution.py:419
  3.0 12.0 %collective-permute-start.2 = (bf16[128,1024]{1,0:T(8,128)(2,1)}, bf16[128,1024]{1,0:T(8,128)(2,1)}, u32[]{:S(2)}, u32[]{:S(2)}) collective-permute-start(bf16[128,1024]{1,0:T(8,128)(2,1)} %q0.1), channel_id=1, source_target_pairs={{0,32},{8,40},{16,48},{24,56},{32,64},{40,72},{48,80},{56,88},{64,... | collective-permute-start | bytes 786440 | tf_op jit(solution)/shard_map/ppermute | solution.py:424
  4.9 15.9 %collective-permute-start.3 = (bf16[128,1024]{1,0:T(8,128)(2,1)}, bf16[128,1024]{1,0:T(8,128)(2,1)}, u32[]{:S(2)}, u32[]{:S(2)}) collective-permute-start(bf16[128,1024]{1,0:T(8,128)(2,1)} %q0.1), channel_id=1, source_target_pairs={{0,64},{8,72},{16,80},{24,88},{32,96},{40,104},{48,112},{56,120},{... | collective-permute-start | bytes 786440 | tf_op jit(solution)/shard_map/ppermute | solution.py:424
  8.5 12.3 %collective-permute-start.4 = (bf16[128,1024]{1,0:T(8,128)(2,1)}, bf16[128,1024]{1,0:T(8,128)(2,1)}, u32[]{:S(2)}, u32[]{:S(2)}) collective-permute-start(bf16[128,1024]{1,0:T(8,128)(2,1)} %q0.1), channel_id=1, source_target_pairs={{0,96},{8,104},{16,112},{24,120},{32,0},{40,8},{48,16},{56,24},{64... | collective-permute-start | bytes 786440 | tf_op jit(solution)/shard_map/ppermute | solution.py:424
  9.5 11.3 %copy-start = (s32[5]{0:T(128)S(1)}, s32[5]{0:T(128)}, u32[]{:S(2)}) copy-start(s32[5]{0:T(128)} %start_ref.5) | copy-start | bytes 64
  20.7 0.7 copy-start.2
  21.4 16.2 %copy-start.1 = (s32[1152]{0:T(1024)S(1)}, s32[1152]{0:T(1024)}, u32[]{:S(2)}) copy-start(s32[1152]{0:T(1024)} %get-tuple-element.33.plan_ref) | copy-start | bytes 13828
  34.8 2.8 %collective-permute-start.5 = (bf16[34,128,128]{2,1,0:T(8,128)(2,1)S(1)}, bf16[34,128,128]{2,1,0:T(8,128)(2,1)S(1)}, u32[]{:S(2)}, u32[]{:S(2)}) collective-permute-start(bf16[34,128,128]{2,1,0:T(8,128)(2,1)S(1)} %collective-permute-done.far_ref), channel_id=1, source_target_pairs={{0,8},{8,0},{16,24},{24,16},{32,40},{40,32},{48,56},{56,48},{64,72... | collective-permute-start | bytes 3342344 | tf_op jit(solution)/shard_map/ppermute | solution.py:419
  37.6 16.2 %copy-start.3 = (s32[8]{0:T(128)S(1)}, s32[8]{0:T(128)}, u32[]{:S(2)}) copy-start(s32[8]{0:T(128)} %constant.11.clone) | copy-start | bytes 100
  51.7 9.5 %collective-permute-start.6 = (bf16[1056,128]{1,0:T(8,128)(2,1)S(1)}, bf16[1056,128]{1,0:T(8,128)(2,1)S(1)}, u32[]{:S(2)}, u32[]{:S(2)}) collective-permute-start(bf16[1056,128]{1,0:T(8,128)(2,1)S(1)} %get-tuple-element.49), channel_id=1, source_target_pairs={{0,96},{8,104},{16,112},{24,120},{32,0},{40,8},{48,16},{56,24},{64... | collective-permute-start | bytes 811016 | tf_op jit(solution)/shard_map/ppermute | solution.py:424
  51.8 11.0 %collective-permute-start.7 = (bf16[1056,128]{1,0:T(8,128)(2,1)S(1)}, bf16[1056,128]{1,0:T(8,128)(2,1)S(1)}, u32[]{:S(2)}, u32[]{:S(2)}) collective-permute-start(bf16[1056,128]{1,0:T(8,128)(2,1)S(1)} %get-tuple-element.50), channel_id=1, source_target_pairs={{0,64},{8,72},{16,80},{24,88},{32,96},{40,104},{48,112},{56,120},{... | collective-permute-start | bytes 811016 | tf_op jit(solution)/shard_map/ppermute | solution.py:424
  52.6 13.9 %collective-permute-start.8 = (bf16[1056,128]{1,0:T(8,128)(2,1)S(1)}, bf16[1056,128]{1,0:T(8,128)(2,1)S(1)}, u32[]{:S(2)}, u32[]{:S(2)}) collective-permute-start(bf16[1056,128]{1,0:T(8,128)(2,1)S(1)} %get-tuple-element.51), channel_id=1, source_target_pairs={{0,32},{8,40},{16,48},{24,56},{32,64},{40,72},{48,80},{56,88},{64,... | collective-permute-start | bytes 811016 | tf_op jit(solution)/shard_map/ppermute | solution.py:424
  67.3 9.8 %collective-permute-start.15 = (bf16[128,1024]{1,0:T(8,128)(2,1)S(1)}, bf16[128,1024]{1,0:T(8,128)(2,1)S(1)}, u32[]{:S(2)}, u32[]{:S(2)}) collective-permute-start(bf16[128,1024]{1,0:T(8,128)(2,1)S(1)} %project.15), channel_id=1, source_target_pairs={{0,1},{1,0},{2,3},{3,2},{4,5},{5,4},{6,7},{7,6},{8,9},{9,8},{10,11... | collective-permute-start | bytes 786440 | tf_op jit(solution)/shard_map/ppermute | solution.py:419
  67.9 16.9 %collective-permute-start.14 = (bf16[128,1024]{1,0:T(8,128)(2,1)S(1)}, bf16[128,1024]{1,0:T(8,128)(2,1)S(1)}, u32[]{:S(2)}, u32[]{:S(2)}) collective-permute-start(bf16[128,1024]{1,0:T(8,128)(2,1)S(1)} %project.14), channel_id=1, source_target_pairs={{0,6},{1,7},{2,4},{3,5},{4,2},{5,3},{6,0},{7,1},{8,14},{9,15},{10,... | collective-permute-start | bytes 786440 | tf_op jit(solution)/shard_map/ppermute | solution.py:419
  71.4 16.6 %collective-permute-start.13 = (bf16[128,1024]{1,0:T(8,128)(2,1)S(1)}, bf16[128,1024]{1,0:T(8,128)(2,1)S(1)}, u32[]{:S(2)}, u32[]{:S(2)}) collective-permute-start(bf16[128,1024]{1,0:T(8,128)(2,1)S(1)} %project.13), channel_id=1, source_target_pairs={{0,2},{1,3},{2,0},{3,1},{4,6},{5,7},{6,4},{7,5},{8,10},{9,11},{10,... | collective-permute-start | bytes 786440 | tf_op jit(solution)/shard_map/ppermute | solution.py:419
  72.1 15.9 %collective-permute-start.12 = (bf16[128,1024]{1,0:T(8,128)(2,1)S(1)}, bf16[128,1024]{1,0:T(8,128)(2,1)S(1)}, u32[]{:S(2)}, u32[]{:S(2)}) collective-permute-start(bf16[128,1024]{1,0:T(8,128)(2,1)S(1)} %project.12), channel_id=1, source_target_pairs={{0,7},{1,6},{2,5},{3,4},{4,3},{5,2},{6,1},{7,0},{8,15},{9,14},{10,... | collective-permute-start | bytes 786440 | tf_op jit(solution)/shard_map/ppermute | solution.py:419
  75.2 12.9 %collective-permute-start.11 = (bf16[128,1024]{1,0:T(8,128)(2,1)S(1)}, bf16[128,1024]{1,0:T(8,128)(2,1)S(1)}, u32[]{:S(2)}, u32[]{:S(2)}) collective-permute-start(bf16[128,1024]{1,0:T(8,128)(2,1)S(1)} %project.11), channel_id=1, source_target_pairs={{0,3},{1,2},{2,1},{3,0},{4,7},{5,6},{6,5},{7,4},{8,11},{9,10},{10,... | collective-permute-start | bytes 786440 | tf_op jit(solution)/shard_map/ppermute | solution.py:419
  77.1 21.3 %collective-permute-start.10 = (bf16[128,1024]{1,0:T(8,128)(2,1)S(1)}, bf16[128,1024]{1,0:T(8,128)(2,1)S(1)}, u32[]{:S(2)}, u32[]{:S(2)}) collective-permute-start(bf16[128,1024]{1,0:T(8,128)(2,1)S(1)} %project.10), channel_id=1, source_target_pairs={{0,4},{1,5},{2,6},{3,7},{4,0},{5,1},{6,2},{7,3},{8,12},{9,13},{10,... | collective-permute-start | bytes 786440 | tf_op jit(solution)/shard_map/ppermute | solution.py:419
  84.7 13.7 %collective-permute-start.9 = (bf16[128,1024]{1,0:T(8,128)(2,1)S(1)}, bf16[128,1024]{1,0:T(8,128)(2,1)S(1)}, u32[]{:S(2)}, u32[]{:S(2)}) collective-permute-start(bf16[128,1024]{1,0:T(8,128)(2,1)S(1)} %project.9), channel_id=1, source_target_pairs={{0,5},{1,4},{2,7},{3,6},{4,1},{5,0},{6,3},{7,2},{8,13},{9,12},{10,... | collective-permute-start | bytes 786440 | tf_op jit(solution)/shard_map/ppermute | solution.py:419
